TPU v7x, 256 devices: a whole 4x4x8 slice. The times are simulated.
256 devices in a mesh: dp: 32 (over y, z_hi, x), seq: 8 (over z_lo, core).
Axes of the slice: x: 4, y: 4, z: 8 (z_hi: 2, z_lo: 4; z = z_hi * 4 + z_lo), core: 2. Of those that a mesh axis runs over, the one named last changes fastest.
Arguments:
- prompt_hidden: bfloat16 [32, 2048, 5120], P('dp', 'seq'), may hold values from -6 to 6
- key_value_weight: bfloat16 [5120, 2048], P(('dp', 'seq')), may hold values from -0.078125 to 0.078125
- key_norm_gain: float32 [1024], replicated, may hold values from 0.25 to 1.75
- page_table: int32 [32, 16], replicated, may hold values from 0 to 15, each once within a row
- lengths: int32 [32], replicated, may hold values from 512 to 2048, as said below
- source_replica: int32 [32], replicated, may hold values from 0 to 31, as said below
- decode_hidden: bfloat16 [3, 512, 5120], P(None, 'dp'), may hold values from -6 to 6
- queries: bfloat16 [3, 512, 5120], P(None, 'dp', 'seq'), may hold values from -1 to 1
Outputs:
- attended: bfloat16 [3, 512, 5120], P(None, 'dp', 'seq')
- forked_cache: float32 [32, 2, 2048, 1024], P('dp', None, None, 'seq')
Inputs may be any that keep to these rules, and one draw needn't show every extreme that they name: `lengths`: some prompt has exactly 2048 tokens and some exactly 512. source_replica[r] is r XOR one nonzero number that is the same for all replicas.
All inputs are finite; a program needn't handle non-finite values.
Results may differ from a plain program's by a relative error of at most 0.0059.
Values may be sent and summed in bfloat16 or wider, within the bound.
A program may use at most 128 MiB of HBM per device.

v0:
```python
import functools
import math

import jax
import jax.numpy as jnp
import numpy as np
from jax import lax
from jax.experimental import pallas as pl
from jax.experimental.pallas import tpu as pltpu
from jax.sharding import PartitionSpec as P

HEADS = 8
HEAD = 128
PAGE = 128
GROUP = 5
MESH = pl.DeviceIdType.MESH
F32 = jnp.float32
BF16 = jnp.bfloat16

WIDTH = 5120
SHARD = 20
PADDED = 32
PAIR_ROWS = 80
BLOCK = 160
TOKENS = 256
CHIP_TOKENS = 512
FRESH = 48
ROWS = CHIP_TOKENS + FRESH
SLAB = CHIP_TOKENS + 16
LANES = 128
UPPER = pl.ds(0, 272)
LOWER = pl.ds(272, 256)


def trig(angle):
    lane = lax.broadcasted_iota(jnp.int32, angle.shape, 1)
    return jnp.cos(angle), jnp.where(lane < HEAD // 2, -jnp.sin(angle), jnp.sin(angle))


def gather_project(
    w_hbm,
    prompt_ref,
    decode_ref,
    table_hbm,
    length_hbm,
    source_hbm,
    freq_hbm,
    gain_hbm,
    pool_ref,
    across_ref,
    stage_ref,
    fresh_ref,
    w_ref,
    table_ref,
    length_ref,
    source_ref,
    freq_ref,
    gain_ref,
    split,
    raw,
    acts,
    weights,
    acc,
    stage,
    squares,
    turns,
    relay,
    send_sem,
    recv_sem,
    local_sem,
):
    dp = lax.axis_index("dp")
    seq = lax.axis_index("seq")
    core = lax.rem(seq, 2)
    z_lo = seq // 2
    x = lax.rem(dp, 4)
    z_hi = lax.rem(dp // 4, 2)
    y = dp // 8
    z = z_hi * 4 + z_lo
    pair = z // 2
    odd = lax.rem(z, 2)

    def at(yy, zz, xx, cc):
        return (yy * 8 + (zz // 4) * 4 + xx, lax.rem(zz, 4) * 2 + cc)

    def turn(index, by, size):
        return lax.rem(index + (by + size), size)

    sibling = at(y, z, x, 1 - core)
    inter_z = turn(z, 2 * odd - 1, 8)
    intra_z = z + 1 - 2 * odd
    inter = at(y, inter_z, x, core)
    intra = at(y, intra_z, x, core)
    intra_other = at(y, intra_z, x, 1 - core)
    rights = {"x": at(y, z, turn(x, 1, 4), core), "y": at(turn(y, 1, 4), z, x, core)}
    lefts = {"x": at(y, z, turn(x, -1, 4), core), "y": at(turn(y, -1, 4), z, x, core)}
    far_chips = [jnp.bitwise_xor(z_lo, d) for d in (1, 2, 3)]
    columns = [(dp, chip * 2 + core) for chip in far_chips]
    opposite = [
        (jnp.bitwise_xor(dp, 4), jnp.bitwise_xor(z_lo, d) * 2 + core) for d in range(4)
    ]

    ahead = at(y, turn(z, 2, 8), x, core)
    behind = at(y, turn(z, -2, 8), x, core)

    peers = opposite[1:] + [
        ahead,
        behind,
        sibling,
        inter,
        intra,
        intra_other,
        rights["x"],
        lefts["x"],
        rights["y"],
        lefts["y"],
        columns[1],
        columns[2],
    ]
    barrier = pltpu.get_barrier_semaphore()
    for peer in peers:
        pl.semaphore_signal(barrier, inc=1, device_id=peer, device_id_type=MESH)

    small = [
        pltpu.make_async_copy(src, dst, local_sem.at[8 + k])
        for k, (src, dst) in enumerate(
            [
                (w_hbm, w_ref),
                (table_hbm, table_ref),
                (length_hbm, length_ref),
                (source_hbm, source_ref),
                (freq_hbm, freq_ref),
                (gain_hbm, gain_ref),
            ]
        )
    ]
    for copy in small:
        copy.start()
    own_acts = pltpu.make_async_copy(
        prompt_ref.at[0],
        acts.at[pl.ds(pl.multiple_of(core * TOKENS, TOKENS), TOKENS)],
        local_sem.at[0],
    )
    own_acts.start()
    own_decode = [
        pltpu.make_async_copy(
            decode_ref.at[step], acts.at[pl.ds(CHIP_TOKENS + step * 16, 16)], local_sem.at[1 + step]
        )
        for step in range(3)
    ]
    for copy in own_decode:
        copy.start()

    for copy in small:
        copy.wait()
    keep = jnp.where(
        lax.broadcasted_iota(jnp.int32, (PADDED, SHARD), 0)
        == lax.broadcasted_iota(jnp.int32, (PADDED, SHARD), 1),
        1.0,
        0.0,
    ).astype(BF16)
    for c in range(2):
        tiles = [
            w_ref[:, pl.ds((1 - g) * HEADS * HEAD + (2 * i + c) * HEAD, HEAD)]
            for g in range(2)
            for i in range(4)
        ]
        split[c] = jnp.dot(
            keep, jnp.concatenate(tiles, axis=1), preferred_element_type=F32
        ).astype(BF16)
    raw[odd * 2 + core] = split[core]
    pl.semaphore_wait(barrier, len(peers))

    number = [0]
    copies = {}

    def send(key, src, dst, device):
        k = number[0]
        number[0] += 1
        copy = pltpu.make_async_remote_copy(
            src_ref=src,
            dst_ref=dst,
            send_sem=send_sem.at[k],
            recv_sem=recv_sem.at[k],
            device_id=device,
            device_id_type=MESH,
        )
        copy.start()
        copies[key] = copy

    def arrived(*keys):
        for key in keys:
            copies[key].wait_recv()

    slot = odd * 2 + core
    mine = split.at[core]
    other = split.at[1 - core]
    send("w_intra", mine, raw.at[slot], intra)
    send("w_other", other, raw.at[slot], intra_other)
    send("w_sibling", other, raw.at[slot], sibling)

    here = pl.ds(pl.multiple_of(core * TOKENS, TOKENS), TOKENS)
    send("acts", prompt_ref.at[0], acts.at[here], sibling)

    arrived("w_intra", "w_other", "w_sibling")
    row = lax.broadcasted_iota(jnp.int32, (PAIR_ROWS, 4 * PADDED), 0)
    col = lax.broadcasted_iota(jnp.int32, (PAIR_ROWS, 4 * PADDED), 1)
    inside = jnp.bitwise_and(col, PADDED - 1)
    source = jnp.right_shift(col, 5)
    pick = jnp.where((row == source * SHARD + inside) & (inside < SHARD), 1.0, 0.0).astype(BF16)
    rows = jnp.dot(
        pick, raw[...].reshape(4 * PADDED, 8 * LANES), preferred_element_type=F32
    ).astype(BF16)

    outer = (y, x)
    inner = (x, y)
    inner_axis = ("x", "y")
    outer_axis = ("y", "x")
    for g in range(2):
        for p in range(2):
            for t in range(2):
                tile = g * 4 + p * 2 + t
                weights[g, p, outer[p], pair, inner[p], pl.ds(t * PAIR_ROWS, PAIR_ROWS)] = rows[
                    :, tile * LANES : (tile + 1) * LANES
                ]

    offsets = (0, -1, 1, 2)
    sign = 2 * odd - 1
    blocks = [pair, turn(pair, sign, 4), turn(pair, -sign, 4), turn(pair, 2, 4)]

    def inner_first(g):
        for p in range(2):
            ref = weights.at[g, p, outer[p], pair, inner[p]]
            send(("i1r", g, p), ref, ref, rights[inner_axis[p]])
            send(("i1l", g, p), ref, ref, lefts[inner_axis[p]])

    def inner_second(g):
        for p in range(2):
            arrived(("i1r", g, p), ("i1l", g, p))
            ref = weights.at[g, p, outer[p], pair]
            low = ref.at[turn(inner[p], -1, 4), pl.ds(0, PAIR_ROWS)]
            high = ref.at[turn(inner[p], 1, 4), pl.ds(PAIR_ROWS, PAIR_ROWS)]
            send(("i2r", g, p), low, low, rights[inner_axis[p]])
            send(("i2l", g, p), high, high, lefts[inner_axis[p]])

    def inner_done(g):
        for p in range(2):
            arrived(("i2r", g, p), ("i2l", g, p))

    def z_step(step, g):
        half = (1 - odd) if step == 3 else odd
        for p in range(2):
            if step >= 2:
                arrived(("z", step - 1, g, p))
            ref = weights.at[g, p, outer[p], blocks[step - 1]]
            if step >= 3:
                ref = ref.at[pl.ds(half * 2, 2)]
            send(("z", step, g, p), ref, ref, inter if step % 2 else intra)

    def z_part(step, part, g):
        half = (1 - odd) if step == 3 else odd
        for p in range(2):
            at_part = turn(inner[p], offsets[part], 4)
            if step >= 2:
                arrived(("zp", step - 1, part, g, p))
            ref = weights.at[g, p, outer[p], blocks[step - 1], at_part]
            if step >= 3:
                ref = ref.at[pl.ds(pl.multiple_of(half * PAIR_ROWS, 16), PAIR_ROWS)]
            send(("zp", step, part, g, p), ref, ref, inter if step % 2 else intra)

    def z_parts_done(g):
        for part in range(4):
            for p in range(2):
                arrived(("zp", 4, part, g, p))

    def z_done(g):
        for p in range(2):
            arrived(("z", 4, g, p))

    def outer_first(block, g):
        for p in range(2):
            ref = weights.at[g, p, outer[p], blocks[block]]
            send(("o1r", block, g, p), ref, ref, rights[outer_axis[p]])
            send(("o1l", block, g, p), ref, ref, lefts[outer_axis[p]])

    def outer_second(block, g):
        for p in range(2):
            arrived(("o1r", block, g, p), ("o1l", block, g, p))
            low = weights.at[g, p, turn(outer[p], -1, 4), blocks[block], pl.ds(0, 2)]
            high = weights.at[g, p, turn(outer[p], 1, 4), blocks[block], pl.ds(2, 2)]
            send(("o2r", block, g, p), low, low, rights[outer_axis[p]])
            send(("o2l", block, g, p), high, high, lefts[outer_axis[p]])

    def own_first(part, g):
        for p in range(2):
            ref = weights.at[g, p, outer[p], pair, turn(inner[p], offsets[part], 4)]
            send(("q1r", part, g, p), ref, ref, rights[outer_axis[p]])
            send(("q1l", part, g, p), ref, ref, lefts[outer_axis[p]])

    def own_second(part, g):
        for p in range(2):
            arrived(("q1r", part, g, p), ("q1l", part, g, p))
            at_part = turn(inner[p], offsets[part], 4)
            low = weights.at[g, p, turn(outer[p], -1, 4), pair, at_part, pl.ds(0, PAIR_ROWS)]
            high = weights.at[
                g, p, turn(outer[p], 1, 4), pair, at_part, pl.ds(PAIR_ROWS, PAIR_ROWS)
            ]
            send(("q2r", part, g, p), low, low, rights[outer_axis[p]])
            send(("q2l", part, g, p), high, high, lefts[outer_axis[p]])

    def outer_done(g):
        for p in range(2):
            if g == 0:
                for part in range(4):
                    arrived(("q2r", part, g, p), ("q2l", part, g, p))
            for block in range(1 - g, 4):
                arrived(("o2r", block, g, p), ("o2l", block, g, p))

    def project(g):
        acc[...] = jnp.zeros_like(acc)

        @pl.loop(0, 4)
        def _(yy):
            left = acts[:, pl.ds(pl.multiple_of(yy * 1280, 1280), 1280)]
            for p in range(2):
                tiles = []
                for t in range(2):
                    pieces = []
                    for zh in range(2):
                        for xx in range(4):
                            for zl in range(2):
                                place = (yy, xx) if p == 0 else (xx, yy)
                                pieces.append(
                                    weights[
                                        g,
                                        p,
                                        place[0],
                                        zh * 2 + zl,
                                        place[1],
                                        pl.ds(t * PAIR_ROWS, PAIR_ROWS),
                                    ]
                                )
                    tiles.append(jnp.concatenate(pieces, axis=0))
                acc[p] += jnp.dot(
                    left, jnp.concatenate(tiles, axis=1), preferred_element_type=F32
                )

    def pack(g):
        peaks = []
        for head in range(4):
            p, lanes = head // 2, pl.ds(head % 2 * LANES, LANES)
            for page in range(4):
                part = pl.ds(page * PAGE, PAGE)
                peaks.append(jnp.max(jnp.abs(acc[p, part, lanes]), axis=0, keepdims=True))
        largest = jnp.max(jnp.concatenate(peaks, axis=0), axis=1, keepdims=True)
        scale = ((largest + 1e-06) / 448.0).astype(BF16).astype(F32)
        inverse = 1.0 / scale
        row = lax.broadcasted_iota(jnp.int32, (16, LANES), 0)
        for head in range(4):
            p, lanes = head // 2, pl.ds(head % 2 * LANES, LANES)
            rows = jnp.zeros((16, LANES), F32)
            for page in range(4):
                part = pl.ds(page * PAGE, PAGE)
                k = head * 4 + page
                stage[g, head, part] = (acc[p, part, lanes] * inverse[k : k + 1]).astype(BF16)
                rows = jnp.where(row == page, scale[k : k + 1], rows)
            stage[g, head, pl.ds(CHIP_TOKENS, 16)] = rows.astype(BF16)

    def all_to_all(g):
        for d in range(3):
            send(
                ("a2a", g, d), stage.at[g, far_chips[d]], pool_ref.at[z_lo], columns[d]
            )
        send(("ahead", 1), stage.at[g, z_lo, UPPER], relay.at[0, UPPER], ahead)
        send(("behind", 1), stage.at[g, z_lo, LOWER], relay.at[1, pl.ds(0, 256)], behind)
        for d in (1, 2, 3):
            send(
                ("across", d),
                stage.at[g, jnp.bitwise_xor(z_lo, d)],
                across_ref.at[z_lo],
                opposite[d],
            )
        own = pltpu.make_async_copy(stage.at[g, z_lo], pool_ref.at[z_lo], local_sem.at[4])
        own.start()
        return own

    def pass_on():
        arrived(("ahead", 1), ("behind", 1))
        place = jnp.bitwise_xor(z_lo, 2)
        send(("ahead", 2), relay.at[0, UPPER], across_ref.at[place, UPPER], ahead)
        send(("behind", 2), relay.at[1, pl.ds(0, 256)], across_ref.at[place, LOWER], behind)

    line = lax.broadcasted_iota(jnp.int32, (PAGE, LANES), 0)
    first = [table_ref[z_lo * 4 + page, dp] * PAGE for page in range(4)]
    own_length = length_ref[dp]

    def live(page):
        return first[page] + line < own_length

    def angles():
        for page in range(4):
            angle = (first[page] + line).astype(F32) * freq_ref[...]
            part = pl.ds(page * PAGE, PAGE)
            turns[0, part], turns[1, part] = trig(angle)
        row = lax.broadcasted_iota(jnp.int32, (FRESH, LANES), 0)
        far_length = length_ref[source_ref[dp]]
        start = jnp.where(jnp.bitwise_and(row, 15) < 8, own_length, far_length)
        angle = (start + jnp.right_shift(row, 4)).astype(F32) * freq_ref[...]
        part = pl.ds(CHIP_TOKENS, FRESH)
        turns[0, part], turns[1, part] = trig(angle)

    tail = pl.ds(CHIP_TOKENS, FRESH)

    def keep_fresh(kind):
        for head in range(4):
            p, lanes = head // 2, pl.ds(head % 2 * LANES, LANES)

            @pl.when(z_lo == head)
            def _():
                fresh_ref[kind] = acc[p, tail, lanes].astype(BF16)

    def values():
        project(0)
        keep_fresh(1)
        for page in range(4):
            part = pl.ds(page * PAGE, PAGE)
            for head in range(4):
                p, lanes = head // 2, pl.ds(head % 2 * LANES, LANES)
                acc[p, part, lanes] = jnp.where(live(page), acc[p, part, lanes], 0.0)
        pack(0)

    def keys():
        project(1)
        total = jnp.zeros((ROWS, 1), F32)
        for p in range(2):
            total += jnp.sum(acc[p] * acc[p], axis=1, keepdims=True)
        squares[0] = jnp.broadcast_to(total, (ROWS, LANES))
        send("squares", squares.at[0], squares.at[1], sibling)
        pass_on()
        parts = [pl.ds(page * PAGE, PAGE) for page in range(4)] + [tail]
        for head in range(4):
            p, lanes = head // 2, pl.ds(head % 2 * LANES, LANES)
            gain = gain_ref[pl.ds(head * 2 + core, 1), :]
            for part in parts:
                row = acc[p, part, lanes] * gain
                acc[p, part, lanes] = row * turns[0, part] + pltpu.roll(row, 64, 1) * turns[1, part]
        arrived("squares")
        for page, part in enumerate(parts):
            norm = lax.rsqrt((squares[0, part] + squares[1, part]) * (1.0 / (HEADS * HEAD)) + 1e-06)
            if page < 4:
                norm = jnp.where(live(page), norm, 0.0)
            for head in range(4):
                p, lanes = head // 2, pl.ds(head % 2 * LANES, LANES)
                acc[p, part, lanes] = acc[p, part, lanes] * norm
        keep_fresh(0)
        pack(1)

    V, K = 0, 1
    inner_first(V)
    z_part(1, 0, V)
    own_first(0, V)
    z_part(1, 0, K)
    inner_first(K)
    inner_second(V)
    z_part(1, 1, V)
    z_part(1, 2, V)
    own_first(1, V)
    own_first(2, V)
    z_part(2, 0, V)
    own_second(0, V)
    inner_done(V)
    z_part(1, 3, V)
    own_first(3, V)
    z_part(2, 0, K)
    own_second(1, V)
    own_second(2, V)
    z_part(3, 0, V)
    z_part(2, 1, V)
    inner_second(K)
    own_second(3, V)
    z_part(2, 2, V)
    z_part(3, 0, K)
    inner_done(K)
    outer_first(0, K)
    z_part(1, 1, K)
    z_part(3, 1, V)
    z_part(2, 3, V)
    outer_first(1, V)
    angles()
    z_part(4, 0, V)
    z_part(3, 2, V)
    z_part(4, 0, K)
    z_part(1, 2, K)
    z_part(3, 3, V)
    outer_first(2, V)
    z_part(2, 1, K)
    z_part(4, 1, V)
    z_part(4, 2, V)
    z_part(1, 3, K)
    z_part(2, 2, K)
    z_part(3, 1, K)
    outer_second(1, V)
    z_part(4, 3, V)
    z_part(2, 3, K)
    z_part(3, 2, K)
    z_part(4, 1, K)
    outer_second(2, V)
    z_parts_done(V)
    outer_first(3, V)
    z_part(4, 2, K)
    z_part(3, 3, K)
    z_part(4, 3, K)
    outer_second(0, K)
    outer_second(3, V)
    outer_first(1, K)
    own_acts.wait()
    for copy in own_decode:
        copy.wait()
    arrived("acts")
    outer_done(V)
    values()
    outer_second(1, K)
    own_values = all_to_all(V)
    outer_first(2, K)
    z_parts_done(K)
    outer_first(3, K)
    outer_second(2, K)
    outer_second(3, K)
    outer_done(K)
    keys()
    stage_keys = pltpu.make_async_copy(stage.at[1], stage_ref, local_sem.at[6])
    stage_keys.start()
    own_values.wait()
    stage_keys.wait()
    for d in range(3):
        arrived(("a2a", V, d))
    for d in (1, 2, 3):
        arrived(("across", d))
    arrived(("ahead", 2), ("behind", 2))
    for copy in copies.values():
        copy.wait_send()


N_COPIES = 4 + 4 * 24 + 2 * 12 + 4 * 12 + 1 + 10


ATTEND_ROWS = GROUP * 3 * 8


def attend(side, q_ref, keys_ref, values_ref, fresh_ref, page_at, length, weight):
    factor = 1.0 / math.sqrt(HEAD)
    steps = 3
    lane = lax.broadcasted_iota(jnp.int32, (1, LANES), 1)
    r = lax.broadcasted_iota(jnp.int32, (ATTEND_ROWS, steps * 8), 0)
    c = lax.broadcasted_iota(jnp.int32, (ATTEND_ROWS, steps * 8), 1)
    visible = (jnp.bitwise_and(r, 7) == jnp.bitwise_and(c, 7)) & (
        jnp.right_shift(lax.rem(r, steps * 8), 3) >= jnp.right_shift(c, 3)
    )
    samples = slice(side * 8, side * 8 + 8)
    query = jnp.concatenate(
        [
            q_ref[:, samples, g * HEAD : (g + 1) * HEAD].astype(F32).reshape(steps * 8, HEAD)
            for g in range(GROUP)
        ],
        axis=0,
    ).astype(BF16)
    new = [
        fresh_ref[kind]
        .astype(F32)
        .reshape(steps, 16, HEAD)[:, samples]
        .reshape(steps * 8, HEAD)
        .astype(BF16)
        for kind in range(2)
    ]
    sums = jnp.zeros((ATTEND_ROWS, LANES), F32)
    for page in range(16):
        chip, part = page // 4, page % 4
        keys = keys_ref[chip, part * PAGE : (part + 1) * PAGE]
        scale = keys_ref[chip, CHIP_TOKENS : CHIP_TOKENS + 16].astype(F32)[part : part + 1]
        raw = lax.dot_general(query, keys, (((1,), (1,)), ((), ())), preferred_element_type=F32)
        live = page_at(page) * PAGE + lane < length
        cached = jnp.where(live, jnp.exp(raw * scale * factor), 0.0)
        weight[:, page * PAGE : (page + 1) * PAGE] = cached
        sums += cached
    fresh_raw = lax.dot_general(
        query, new[0], (((1,), (1,)), ((), ())), preferred_element_type=F32
    )
    fresh = jnp.where(visible, jnp.exp(fresh_raw * factor), 0.0)
    total = jnp.sum(sums, axis=1, keepdims=True) + jnp.sum(fresh, axis=1, keepdims=True)
    result = jnp.dot((fresh / total).astype(BF16), new[1], preferred_element_type=F32)
    for page in range(16):
        chip, part = page // 4, page % 4
        scale = values_ref[chip, CHIP_TOKENS : CHIP_TOKENS + 16].astype(F32)[part : part + 1]
        portion = weight[:, page * PAGE : (page + 1) * PAGE] / total * scale
        result += jnp.dot(
            portion.astype(BF16),
            values_ref[chip, part * PAGE : (part + 1) * PAGE],
            preferred_element_type=F32,
        )
    return [
        result[g * steps * 8 : (g + 1) * steps * 8].reshape(steps, 8, HEAD) for g in range(GROUP)
    ]


def exchange(
    mask, pool_ref, across_ref, stage_ref, far_ref, keys_ref, send_sem, recv_sem, local_sem
):
    dp = lax.axis_index("dp")
    seq = lax.axis_index("seq")
    core = lax.rem(seq, 2)
    z_lo = seq // 2
    partner = jnp.bitwise_xor(dp, mask)
    far_chips = [jnp.bitwise_xor(z_lo, d) for d in (1, 2, 3)]
    columns = [(dp, chip * 2 + core) for chip in far_chips]
    partners = [(partner, jnp.bitwise_xor(z_lo, d) * 2 + core) for d in range(4)]
    plane = mask & ~4
    held = across_ref if mask & 4 else pool_ref
    holder = (jnp.bitwise_xor(dp, plane), seq)

    peers = columns + partners
    if plane and mask & 4:
        peers = peers + [holder]
    barrier = pltpu.get_barrier_semaphore()
    for peer in peers:
        pl.semaphore_signal(barrier, inc=1, device_id=peer, device_id_type=MESH)
    own = pltpu.make_async_copy(stage_ref.at[z_lo], keys_ref.at[z_lo], local_sem.at[0])
    own.start()
    pl.semaphore_wait(barrier, len(peers))

    copies = []

    def send(src, dst, device):
        k = len(copies)
        copy = pltpu.make_async_remote_copy(
            src_ref=src,
            dst_ref=dst,
            send_sem=send_sem.at[k],
            recv_sem=recv_sem.at[k],
            device_id=device,
            device_id_type=MESH,
        )
        copy.start()
        copies.append(copy)

    for d in range(4):
        send(stage_ref.at[jnp.bitwise_xor(z_lo, d)], far_ref.at[0, z_lo], partners[d])
    if plane:
        send(held, far_ref.at[1], holder)
    else:
        local = pltpu.make_async_copy(held, far_ref.at[1], local_sem.at[1])
        local.start()
        local.wait()
    for d in (1, 2, 3):
        send(stage_ref.at[far_chips[d - 1]], keys_ref.at[z_lo], columns[d - 1])
    own.wait()
    for copy in copies:
        copy.wait()


def finish(
    q_ref,
    table_ref,
    length_ref,
    source_ref,
    keys_ref,
    values_ref,
    far_ref,
    fresh_ref,
    out_ref,
    fork_ref,
    weight,
):
    dp = lax.axis_index("dp")
    partner = source_ref[dp]
    near = attend(
        0,
        q_ref,
        keys_ref,
        values_ref,
        fresh_ref,
        lambda page: table_ref[page, dp],
        length_ref[dp],
        weight,
    )
    far = attend(
        1,
        q_ref,
        far_ref.at[0],
        far_ref.at[1],
        fresh_ref,
        lambda page: table_ref[page, partner],
        length_ref[partner],
        weight,
    )
    for g in range(GROUP):
        span = slice(g * HEAD, (g + 1) * HEAD)
        out_ref[:, :, span] = jnp.concatenate([near[g], far[g]], axis=1).astype(BF16)
    for kind in range(2):
        for page in range(16):
            chip, part = page // 4, page % 4
            scale = far_ref[kind, chip, CHIP_TOKENS : CHIP_TOKENS + 16].astype(F32)[
                part : part + 1
            ]
            fork_ref[0, kind, page * PAGE : (page + 1) * PAGE] = (
                far_ref[kind, chip, part * PAGE : (part + 1) * PAGE].astype(F32) * scale
            )


def on_device(
    prompt_hidden,
    key_value_weight,
    key_norm_gain,
    page_table,
    lengths,
    source_replica,
    decode_hidden,
    queries,
):
    steps, paired, width = queries.shape
    replicas = lax.axis_size("dp")
    table = page_table.T
    freq = 500000.0 ** (-np.arange(HEAD // 2) * 2.0 / HEAD)
    freq = jnp.asarray(np.concatenate([freq, freq])[None].astype(np.float32))

    vmem = pl.BlockSpec(memory_space=pltpu.VMEM)
    smem = pl.BlockSpec(memory_space=pltpu.SMEM)
    hbm = pl.BlockSpec(memory_space=pl.ANY)
    pinned = pl.BlockSpec(memory_space=pltpu.HBM)
    pool, across, stage, fresh = pl.pallas_call(
        gather_project,
        out_shape=(
            jax.ShapeDtypeStruct((4, SLAB, LANES), BF16),
            jax.ShapeDtypeStruct((4, SLAB, LANES), BF16),
            jax.ShapeDtypeStruct((4, SLAB, LANES), BF16),
            jax.ShapeDtypeStruct((2, FRESH, LANES), BF16),
        ),
        in_specs=[pinned] * 8,
        out_specs=(hbm, hbm, hbm, vmem),
        scratch_shapes=[
            pltpu.VMEM((SHARD, 2 * HEADS * HEAD), BF16),
            pltpu.SMEM((16, 32), jnp.int32),
            pltpu.SMEM((32,), jnp.int32),
            pltpu.SMEM((32,), jnp.int32),
            pltpu.VMEM((1, LANES), F32),
            pltpu.VMEM((HEADS, HEAD), F32),
            pltpu.VMEM((2, PADDED, 8 * LANES), BF16),
            pltpu.VMEM((4, PADDED, 8 * LANES), BF16),
            pltpu.VMEM((ROWS, WIDTH), BF16),
            pltpu.VMEM((2, 2, 4, 4, 4, BLOCK, LANES), BF16),
            pltpu.VMEM((2, ROWS, 2 * LANES), F32),
            pltpu.VMEM((2, 4, SLAB, LANES), BF16),
            pltpu.VMEM((2, ROWS, LANES), F32),
            pltpu.VMEM((2, ROWS, LANES), F32),
            pltpu.VMEM((2, 272, LANES), BF16),
            pltpu.SemaphoreType.DMA((N_COPIES,)),
            pltpu.SemaphoreType.DMA((N_COPIES,)),
            pltpu.SemaphoreType.DMA((16,)),
        ],
        compiler_params=pltpu.CompilerParams(
            collective_id=0, has_side_effects=True, vmem_limit_bytes=44 * 1024 * 1024
        ),
    )(
        key_value_weight,
        prompt_hidden,
        decode_hidden,
        table,
        lengths,
        source_replica,
        freq,
        key_norm_gain.reshape(HEADS, HEAD),
    )

    def exchange_by(mask):
        return pl.pallas_call(
            functools.partial(exchange, mask),
            out_shape=(
                jax.ShapeDtypeStruct((2, 4, SLAB, LANES), BF16),
                jax.ShapeDtypeStruct((4, SLAB, LANES), BF16),
            ),
            in_specs=[hbm, hbm, hbm],
            out_specs=(hbm, hbm),
            scratch_shapes=[
                pltpu.SemaphoreType.DMA((8,)),
                pltpu.SemaphoreType.DMA((8,)),
                pltpu.SemaphoreType.DMA((2,)),
            ],
            compiler_params=pltpu.CompilerParams(collective_id=mask, has_side_effects=True),
        )

    far_pool, near_keys = lax.switch(
        source_replica[0] - 1,
        [exchange_by(mask) for mask in range(1, replicas)],
        pool,
        across,
        stage,
    )

    attended, forked = pl.pallas_call(
        finish,
        out_shape=(
            jax.ShapeDtypeStruct((steps, paired, width), BF16),
            jax.ShapeDtypeStruct((1, 2, 2048, LANES), F32),
        ),
        in_specs=[vmem, smem, smem, smem, vmem, vmem, vmem, vmem],
        out_specs=(vmem, vmem),
        scratch_shapes=[pltpu.VMEM((ATTEND_ROWS, 2048), F32)],
        compiler_params=pltpu.CompilerParams(vmem_limit_bytes=32 * 1024 * 1024),
    )(queries, table, lengths, source_replica, near_keys, pool, far_pool, fresh)
    return attended, forked


def solution(mesh):
    return jax.shard_map(
        on_device,
        mesh=mesh,
        in_specs=(
            P("dp", "seq", None),
            P(("dp", "seq"), None),
            P(),
            P(),
            P(),
            P(),
            P(None, "dp", None),
            P(None, "dp", "seq"),
        ),
        out_specs=(P(None, "dp", "seq"), P("dp", None, None, "seq")),
        check_vma=False,
    )
```

profile of v0, /device:TPU:6, one launch (start us, length us, event | category | flops | bytes accessed | tf_op | source)
XLA Modules:
  0.0 122.8 jit_solution(9618858372374648149)
XLA Ops:
  1.3 0.0 copy-start
  1.3 1.7 %copy-done = bf16[1,256,5120]{2,1,0:T(8,128)(2,1)S(1)} copy-done((bf16[1,256,5120]{2,1,0:T(8,128)(2,1)S(1)}, bf16[1,256,5120]{2,1,0:T(8,128)(2,1)}, u32[]{:S(2)}) %copy-start) | copy-done | bytes 2621464
  3.0 0.0 copy-start.1
  3.0 1.0 copy-done.1
  4.1 0.9 copy-done.2
  4.9 0.0 copy-start.4
  4.9 0.7 copy-done.4
  5.6 0.0 copy-start.6
  5.6 0.7 copy-done.6
  6.3 0.7 copy-done.7
  7.0 0.7 copy-done.9
  7.6 0.7 copy-done.11
  8.3 81.9 %shard_map.104 = (bf16[4,528,128]{2,1,0:T(8,128)(2,1)S(1)}, bf16[4,528,128]{2,1,0:T(8,128)(2,1)S(1)}, bf16[4,528,128]{2,1,0:T(8,128)(2,1)S(1)}, bf16[2,48,128]{2,1,0:T(8,128)(2,1)S(1)}) custom-call(bf16[20,2048]{1,0:T(8,128)(2,1)S(1)} %copy-done.2, bf16[1,256,5120]{2,1,0:T(8,128)(2,1)S(1)} %copy-done, bf16[3,16,5120]{2,1,0:T(8,128)(2,1)S(1)} %copy-done.1, ...), custom_call_target="tpu_custom_call" | custom-call | tf_op jit(solution)/shard_map/pallas_call | solution.py:729
  90.2 0.0 copy-start.3
  90.2 0.0 copy-start.5
  90.2 0.0 copy-start.8
  90.2 0.0 copy-start.10
  90.3 28.6 %conditional.1 = ((bf16[2,4,528,128]{3,2,1,0:T(8,128)(2,1)S(1)}, bf16[4,528,128]{2,1,0:T(8,128)(2,1)S(1)})) conditional(s32[]{:T(128)} %bitcast.1, (bf16[4,528,128]{2,1,0:T(8,128)(2,1)S(1)}, bf16[4,528,128]{2,1,0:T(8,128)(2,1)S(1)}, bf16[4,528,128]{2,1,0:T(8,128)(2,1)S(1)}) %tuple.100, ...), branch_computations={%region_0.0_spmd, %region_1.0_spmd, %region_2.0_spmd, %region_3.0_... | conditional | bytes 8 | solution.py:790
  90.3 28.3 %branch_14_fun.1 = (bf16[2,4,528,128]{3,2,1,0:T(8,128)(2,1)S(1)}, bf16[4,528,128]{2,1,0:T(8,128)(2,1)S(1)}) custom-call(bf16[4,528,128]{2,1,0:T(8,128)(2,1)S(1)} %get-tuple-element.228.pool_ref, bf16[4,528,128]{2,1,0:T(8,128)(2,1)S(1)} %get-tuple-element.229.across_ref, bf16[4,528,128]{2,1,0:T(8,128)(2,1)S(1)} %get-tuple-element.230.stage_ref), custom_call_target="tpu_custom_call" | custom-call | tf_op jit(solution)/shard_map/cond/branch_14_fun/pallas_call | solution.py:790
  118.8 0.0 copy-done.3
  118.9 0.0 copy-done.5
  118.9 0.0 copy-done.8
  118.9 0.0 copy-done.10
  118.9 3.9 %shard_map.105 = (bf16[3,16,640]{2,1,0:T(8,128)(2,1)}, f32[1,2,2048,128]{3,2,1,0:T(8,128)}) custom-call(bf16[3,16,640]{2,1,0:T(8,128)(2,1)S(1)} %copy-done.3, s32[16,32]{1,0:T(8,128)S(1)} %bitcast.5, s32[32]{0:T(128)S(1)} %copy-done.8, s32[32]{0:T(128)S(1)} %copy-done.10, bf16[4,528,128]{2,1,0:T(8,128)(2,1)S(1)} %get-tuple-element.290.keys_ref, ...), custom_call_target="tpu_custom_call" | custom-call | tf_op jit(solution)/shard_map/pallas_call | solution.py:798
  (4 shorter events, 0.0 us)
Async XLA Ops:
  1.3 1.7 %copy-start = (bf16[1,256,5120]{2,1,0:T(8,128)(2,1)S(1)}, bf16[1,256,5120]{2,1,0:T(8,128)(2,1)}, u32[]{:S(2)}) copy-start(bf16[1,256,5120]{2,1,0:T(8,128)(2,1)} %prompt_ref.1) | copy-start | bytes 7864324
  3.0 1.0 copy-start.1
  4.1 0.9 copy-start.2
  4.9 0.7 copy-start.4
  5.6 0.7 copy-start.6
  6.3 0.7 copy-start.7
  7.0 0.7 copy-start.9
  7.6 0.7 copy-start.11
  90.2 28.6 %copy-start.3 = (bf16[3,16,640]{2,1,0:T(8,128)(2,1)S(1)}, bf16[3,16,640]{2,1,0:T(8,128)(2,1)}, u32[]{:S(2)}) copy-start(bf16[3,16,640]{2,1,0:T(8,128)(2,1)} %q_ref.1) | copy-start | bytes 184324
  90.2 28.6 %copy-start.5 = (s32[32,16]{0,1:T(8,128)S(1)}, s32[32,16]{0,1:T(8,128)}, u32[]{:S(2)}) copy-start(s32[32,16]{0,1:T(8,128)} %param.43) | copy-start | bytes 6148
  90.2 28.6 %copy-start.8 = (s32[32]{0:T(128)S(1)}, s32[32]{0:T(128)}, u32[]{:S(2)}) copy-start(s32[32]{0:T(128)} %length_ref.1) | copy-start | bytes 388
  90.2 28.6 %copy-start.10 = (s32[32]{0:T(128)S(1)}, s32[32]{0:T(128)}, u32[]{:S(2)}) copy-start(s32[32]{0:T(128)} %source_ref.1) | copy-start | bytes 388
where the time goes:
time: 125 us; the launch traced here: 123 us
  Pallas kernels  114 us (91%)
  local copies, waits for them, and re-layouts  7.03 us (6%)
  between operations  1.38 us (1%)
    pallas_call x1, Pallas kernels, on_device(): pl.pallas_call(gather_project, out_shape=(jax.ShapeDtypeStruct((4, SLAB,...  81.9 us
    pallas_call x1, Pallas kernels, on_device(): lax.switch(source_replica[0] - 1, [exchange_by(mask) for mask in range(1,...  28.3 us
    unnamed x24, local copies, waits for them, and re-layouts  7.03 us
    pallas_call x1, Pallas kernels, on_device(): pl.pallas_call(finish, out_shape=(jax.ShapeDtypeStruct((steps, paired, wi...  3.89 us

commit v1 on v0

--- a/solution.py
+++ b/solution.py
@@ -151,24 +151,22 @@
     for copy in own_decode:
         copy.start()
 
-    for copy in small:
-        copy.wait()
+    small[0].wait()
     keep = jnp.where(
         lax.broadcasted_iota(jnp.int32, (PADDED, SHARD), 0)
         == lax.broadcasted_iota(jnp.int32, (PADDED, SHARD), 1),
         1.0,
         0.0,
     ).astype(BF16)
-    for c in range(2):
-        tiles = [
-            w_ref[:, pl.ds((1 - g) * HEADS * HEAD + (2 * i + c) * HEAD, HEAD)]
-            for g in range(2)
-            for i in range(4)
-        ]
-        split[c] = jnp.dot(
-            keep, jnp.concatenate(tiles, axis=1), preferred_element_type=F32
-        ).astype(BF16)
-    raw[odd * 2 + core] = split[core]
+    for g in range(2):
+        for c in range(2):
+            tiles = [
+                w_ref[:, pl.ds((1 - g) * HEADS * HEAD + (2 * i + c) * HEAD, HEAD)] for i in range(4)
+            ]
+            split[g, c] = jnp.dot(
+                keep, jnp.concatenate(tiles, axis=1), preferred_element_type=F32
+            ).astype(BF16)
+        raw[g, odd * 2 + core] = split[g, core]
     pl.semaphore_wait(barrier, len(peers))
 
     number = [0]
@@ -193,33 +191,33 @@
             copies[key].wait_recv()
 
     slot = odd * 2 + core
-    mine = split.at[core]
-    other = split.at[1 - core]
-    send("w_intra", mine, raw.at[slot], intra)
-    send("w_other", other, raw.at[slot], intra_other)
-    send("w_sibling", other, raw.at[slot], sibling)
+    for g in range(2):
+        send(("w_intra", g), split.at[g, core], raw.at[g, slot], intra)
+        send(("w_other", g), split.at[g, 1 - core], raw.at[g, slot], intra_other)
+        send(("w_sibling", g), split.at[g, 1 - core], raw.at[g, slot], sibling)
 
     here = pl.ds(pl.multiple_of(core * TOKENS, TOKENS), TOKENS)
     send("acts", prompt_ref.at[0], acts.at[here], sibling)
 
-    arrived("w_intra", "w_other", "w_sibling")
     row = lax.broadcasted_iota(jnp.int32, (PAIR_ROWS, 4 * PADDED), 0)
     col = lax.broadcasted_iota(jnp.int32, (PAIR_ROWS, 4 * PADDED), 1)
     inside = jnp.bitwise_and(col, PADDED - 1)
     source = jnp.right_shift(col, 5)
     pick = jnp.where((row == source * SHARD + inside) & (inside < SHARD), 1.0, 0.0).astype(BF16)
-    rows = jnp.dot(
-        pick, raw[...].reshape(4 * PADDED, 8 * LANES), preferred_element_type=F32
-    ).astype(BF16)
 
     outer = (y, x)
     inner = (x, y)
     inner_axis = ("x", "y")
     outer_axis = ("y", "x")
-    for g in range(2):
+
+    def assemble(g):
+        arrived(("w_intra", g), ("w_other", g), ("w_sibling", g))
+        rows = jnp.dot(
+            pick, raw[g].reshape(4 * PADDED, 4 * LANES), preferred_element_type=F32
+        ).astype(BF16)
         for p in range(2):
             for t in range(2):
-                tile = g * 4 + p * 2 + t
+                tile = p * 2 + t
                 weights[g, p, outer[p], pair, inner[p], pl.ds(t * PAIR_ROWS, PAIR_ROWS)] = rows[
                     :, tile * LANES : (tile + 1) * LANES
                 ]
@@ -316,34 +314,46 @@
             for block in range(1 - g, 4):
                 arrived(("o2r", block, g, p), ("o2l", block, g, p))
 
+    def add(g, p, yy, fresh=False):
+        tiles = []
+        for t in range(2):
+            pieces = []
+            for zh in range(2):
+                for xx in range(4):
+                    for zl in range(2):
+                        place = (yy, xx) if p == 0 else (xx, yy)
+                        pieces.append(
+                            weights[
+                                g,
+                                p,
+                                place[0],
+                                zh * 2 + zl,
+                                place[1],
+                                pl.ds(t * PAIR_ROWS, PAIR_ROWS),
+                            ]
+                        )
+            tiles.append(jnp.concatenate(pieces, axis=0))
+        product = jnp.dot(
+            acts[:, pl.ds(pl.multiple_of(yy * 1280, 1280), 1280)],
+            jnp.concatenate(tiles, axis=1),
+            preferred_element_type=F32,
+        )
+        acc[p] = product if fresh else acc[p] + product
+
+    def project_early(g):
+        add(g, 0, y, True)
+
+        @pl.loop(0, 2)
+        def _(k):
+            add(g, 0, lax.rem(y + 1 + 2 * k, 4))
+
     def project(g):
-        acc[...] = jnp.zeros_like(acc)
-
-        @pl.loop(0, 4)
+        add(g, 0, turn(y, 2, 4))
+        add(g, 1, 0, True)
+
+        @pl.loop(1, 4)
         def _(yy):
-            left = acts[:, pl.ds(pl.multiple_of(yy * 1280, 1280), 1280)]
-            for p in range(2):
-                tiles = []
-                for t in range(2):
-                    pieces = []
-                    for zh in range(2):
-                        for xx in range(4):
-                            for zl in range(2):
-                                place = (yy, xx) if p == 0 else (xx, yy)
-                                pieces.append(
-                                    weights[
-                                        g,
-                                        p,
-                                        place[0],
-                                        zh * 2 + zl,
-                                        place[1],
-                                        pl.ds(t * PAIR_ROWS, PAIR_ROWS),
-                                    ]
-                                )
-                    tiles.append(jnp.concatenate(pieces, axis=0))
-                acc[p] += jnp.dot(
-                    left, jnp.concatenate(tiles, axis=1), preferred_element_type=F32
-                )
+            add(g, 1, yy)
 
     def pack(g):
         peaks = []
@@ -391,20 +401,22 @@
         send(("behind", 2), relay.at[1, pl.ds(0, 256)], across_ref.at[place, LOWER], behind)
 
     line = lax.broadcasted_iota(jnp.int32, (PAGE, LANES), 0)
-    first = [table_ref[z_lo * 4 + page, dp] * PAGE for page in range(4)]
-    own_length = length_ref[dp]
+    def first(page):
+        return table_ref[z_lo * 4 + page, dp] * PAGE
 
     def live(page):
-        return first[page] + line < own_length
+        return first(page) + line < length_ref[dp]
 
     def angles():
+        for copy in small[1:]:
+            copy.wait()
         for page in range(4):
-            angle = (first[page] + line).astype(F32) * freq_ref[...]
+            angle = (first(page) + line).astype(F32) * freq_ref[...]
             part = pl.ds(page * PAGE, PAGE)
             turns[0, part], turns[1, part] = trig(angle)
         row = lax.broadcasted_iota(jnp.int32, (FRESH, LANES), 0)
         far_length = length_ref[source_ref[dp]]
-        start = jnp.where(jnp.bitwise_and(row, 15) < 8, own_length, far_length)
+        start = jnp.where(jnp.bitwise_and(row, 15) < 8, length_ref[dp], far_length)
         angle = (start + jnp.right_shift(row, 4)).astype(F32) * freq_ref[...]
         part = pl.ds(CHIP_TOKENS, FRESH)
         turns[0, part], turns[1, part] = trig(angle)
@@ -456,9 +468,11 @@
         pack(1)
 
     V, K = 0, 1
+    assemble(V)
     inner_first(V)
     z_part(1, 0, V)
     own_first(0, V)
+    assemble(K)
     z_part(1, 0, K)
     inner_first(K)
     inner_second(V)
@@ -517,6 +531,7 @@
     for copy in own_decode:
         copy.wait()
     arrived("acts")
+    project_early(V)
     outer_done(V)
     values()
     outer_second(1, K)
@@ -526,6 +541,7 @@
     outer_first(3, K)
     outer_second(2, K)
     outer_second(3, K)
+    project_early(K)
     outer_done(K)
     keys()
     stage_keys = pltpu.make_async_copy(stage.at[1], stage_ref, local_sem.at[6])
@@ -541,7 +557,7 @@
         copy.wait_send()
 
 
-N_COPIES = 4 + 4 * 24 + 2 * 12 + 4 * 12 + 1 + 10
+N_COPIES = 7 + 4 * 24 + 2 * 12 + 4 * 12 + 1 + 10
 
 
 ATTEND_ROWS = GROUP * 3 * 8
@@ -642,8 +658,6 @@
         copy.start()
         copies.append(copy)
 
-    for d in range(4):
-        send(stage_ref.at[jnp.bitwise_xor(z_lo, d)], far_ref.at[0, z_lo], partners[d])
     if plane:
         send(held, far_ref.at[1], holder)
     else:
@@ -652,6 +666,8 @@
         local.wait()
     for d in (1, 2, 3):
         send(stage_ref.at[far_chips[d - 1]], keys_ref.at[z_lo], columns[d - 1])
+    for d in (3, 2, 1, 0):
+        send(stage_ref.at[jnp.bitwise_xor(z_lo, d)], far_ref.at[0, z_lo], partners[d])
     own.wait()
     for copy in copies:
         copy.wait()
@@ -743,8 +759,8 @@
             pltpu.SMEM((32,), jnp.int32),
             pltpu.VMEM((1, LANES), F32),
             pltpu.VMEM((HEADS, HEAD), F32),
-            pltpu.VMEM((2, PADDED, 8 * LANES), BF16),
-            pltpu.VMEM((4, PADDED, 8 * LANES), BF16),
+            pltpu.VMEM((2, 2, PADDED, 4 * LANES), BF16),
+            pltpu.VMEM((2, 4, PADDED, 4 * LANES), BF16),
             pltpu.VMEM((ROWS, WIDTH), BF16),
             pltpu.VMEM((2, 2, 4, 4, 4, BLOCK, LANES), BF16),
             pltpu.VMEM((2, ROWS, 2 * LANES), F32),
@@ -757,7 +773,7 @@
             pltpu.SemaphoreType.DMA((16,)),
         ],
         compiler_params=pltpu.CompilerParams(
-            collective_id=0, has_side_effects=True, vmem_limit_bytes=44 * 1024 * 1024
+            collective_id=0, has_side_effects=True, vmem_limit_bytes=60 * 1024 * 1024
         ),
     )(
         key_value_weight,

time: 125 us -> 111 us (0.89); the launches traced: 123 us -> 111 us
  local copies, waits for them, and re-layouts: 7.03 us -> 0.03 us
  Pallas kernels: 114 us -> 110 us
    unnamed x24 -> x10, local copies, waits for them, and re-layouts: 7.03 us -> 0.03 us
    pallas_call x1, Pallas kernels: 28.3 us -> 24.6 us  [on_device(): lax.switch(source_replica[0] - 1, [exchange_by(mask) for mask in range(1,...]
where the time goes in v1:
time: 111 us
  Pallas kernels  110 us (99%)
  between operations  1.38 us (1%)
    pallas_call x1, Pallas kernels, on_device(): pl.pallas_call(gather_project, out_shape=(jax.ShapeDtypeStruct((4, SLAB,...  81.2 us
    pallas_call x1, Pallas kernels, on_device(): lax.switch(source_replica[0] - 1, [exchange_by(mask) for mask in range(1,...  24.6 us
    pallas_call x1, Pallas kernels, on_device(): pl.pallas_call(finish, out_shape=(jax.ShapeDtypeStruct((steps, paired, wi...  3.89 us

profile of v1, /device:TPU:6, one launch (start us, length us, event | category | flops | bytes accessed | tf_op | source)
XLA Modules:
  0.0 111.3 jit_solution(3646592444104674950)
XLA Ops:
  1.3 81.2 %shard_map.104 = (bf16[4,528,128]{2,1,0:T(8,128)(2,1)S(1)}, bf16[4,528,128]{2,1,0:T(8,128)(2,1)S(1)}, bf16[4,528,128]{2,1,0:T(8,128)(2,1)S(1)}, bf16[2,48,128]{2,1,0:T(8,128)(2,1)}) custom-call(bf16[20,2048]{1,0:T(8,128)(2,1)} %w_hbm.1, bf16[1,256,5120]{2,1,0:T(8,128)(2,1)} %prompt_ref.1, bf16[3,16,5120]{2,1,0:T(8,128)(2,1)} %decode_ref.1, ...), custom_call_target="tpu_custom_call" | custom-call | tf_op jit(solution)/shard_map/pallas_call | solution.py:745
  82.5 0.0 copy-start
  82.5 0.0 copy-start.1
  82.5 0.0 copy-start.2
  82.5 0.0 copy-start.3
  82.5 0.0 copy-start.4
  82.6 24.8 %conditional.1 = ((bf16[2,4,528,128]{3,2,1,0:T(8,128)(2,1)S(1)}, bf16[4,528,128]{2,1,0:T(8,128)(2,1)S(1)})) conditional(s32[]{:T(128)} %bitcast.1, (bf16[4,528,128]{2,1,0:T(8,128)(2,1)S(1)}, bf16[4,528,128]{2,1,0:T(8,128)(2,1)S(1)}, bf16[4,528,128]{2,1,0:T(8,128)(2,1)S(1)}) %tuple.100, ...), branch_computations={%region_0.0_spmd, %region_1.0_spmd, %region_2.0_spmd, %region_3.0_... | conditional | bytes 8 | solution.py:806
  82.6 24.6 %branch_7_fun.1 = (bf16[2,4,528,128]{3,2,1,0:T(8,128)(2,1)S(1)}, bf16[4,528,128]{2,1,0:T(8,128)(2,1)S(1)}) custom-call(bf16[4,528,128]{2,1,0:T(8,128)(2,1)S(1)} %get-tuple-element.207.pool_ref, bf16[4,528,128]{2,1,0:T(8,128)(2,1)S(1)} %get-tuple-element.208.across_ref, bf16[4,528,128]{2,1,0:T(8,128)(2,1)S(1)} %get-tuple-element.209.stage_ref), custom_call_target="tpu_custom_call" | custom-call | tf_op jit(solution)/shard_map/cond/branch_7_fun/pallas_call | solution.py:806
  107.4 0.0 copy-done
  107.4 0.0 copy-done.1
  107.4 0.0 copy-done.2
  107.4 0.0 copy-done.3
  107.4 0.0 copy-done.4
  107.4 3.9 %shard_map.105 = (bf16[3,16,640]{2,1,0:T(8,128)(2,1)}, f32[1,2,2048,128]{3,2,1,0:T(8,128)}) custom-call(bf16[3,16,640]{2,1,0:T(8,128)(2,1)S(1)} %copy-done, s32[16,32]{1,0:T(8,128)S(1)} %bitcast.5, s32[32]{0:T(128)S(1)} %copy-done.3, s32[32]{0:T(128)S(1)} %copy-done.4, bf16[4,528,128]{2,1,0:T(8,128)(2,1)S(1)} %get-tuple-element.290.keys_ref, ...), custom_call_target="tpu_custom_call" | custom-call | tf_op jit(solution)/shard_map/pallas_call | solution.py:814
Async XLA Ops:
  82.5 24.9 %copy-start = (bf16[3,16,640]{2,1,0:T(8,128)(2,1)S(1)}, bf16[3,16,640]{2,1,0:T(8,128)(2,1)}, u32[]{:S(2)}) copy-start(bf16[3,16,640]{2,1,0:T(8,128)(2,1)} %q_ref.1) | copy-start | bytes 184324
  82.5 24.9 %copy-start.1 = (s32[32,16]{0,1:T(8,128)S(1)}, s32[32,16]{0,1:T(8,128)}, u32[]{:S(2)}) copy-start(s32[32,16]{0,1:T(8,128)} %param.43) | copy-start | bytes 6148
  82.5 24.9 %copy-start.2 = (bf16[2,48,128]{2,1,0:T(8,128)(2,1)S(1)}, bf16[2,48,128]{2,1,0:T(8,128)(2,1)}, u32[]{:S(2)}) copy-start(bf16[2,48,128]{2,1,0:T(8,128)(2,1)} %get-tuple-element.292.fresh_ref) | copy-start | bytes 73732
  82.5 24.9 %copy-start.3 = (s32[32]{0:T(128)S(1)}, s32[32]{0:T(128)}, u32[]{:S(2)}) copy-start(s32[32]{0:T(128)} %length_ref.1) | copy-start | bytes 388
  82.5 24.9 %copy-start.4 = (s32[32]{0:T(128)S(1)}, s32[32]{0:T(128)}, u32[]{:S(2)}) copy-start(s32[32]{0:T(128)} %source_ref.1) | copy-start | bytes 388

commit v2 on v1

--- a/solution.py
+++ b/solution.py
@@ -59,6 +59,7 @@
     split,
     raw,
     acts,
+    acts_x,
     weights,
     acc,
     stage,
@@ -314,48 +315,50 @@
             for block in range(1 - g, 4):
                 arrived(("o2r", block, g, p), ("o2l", block, g, p))
 
-    def add(g, p, yy, fresh=False):
+    def by_x(piece):
+        part = pl.ds(piece * 112, 112)
+        for xx in range(4):
+            acts_x[xx, part] = jnp.concatenate(
+                [
+                    acts[part, pl.ds(yz * 640, 640)][:, xx * 160 : (xx + 1) * 160]
+                    for yz in range(8)
+                ],
+                axis=1,
+            )
+
+    def add(g, p, at_outer, fresh=False):
         tiles = []
         for t in range(2):
             pieces = []
-            for zh in range(2):
-                for xx in range(4):
+            for i in range(4):
+                for zh in range(2):
                     for zl in range(2):
-                        place = (yy, xx) if p == 0 else (xx, yy)
-                        pieces.append(
-                            weights[
-                                g,
-                                p,
-                                place[0],
-                                zh * 2 + zl,
-                                place[1],
-                                pl.ds(t * PAIR_ROWS, PAIR_ROWS),
-                            ]
-                        )
+                        part = pl.ds(t * PAIR_ROWS, PAIR_ROWS)
+                        pieces.append(weights[g, p, at_outer, zh * 2 + zl, i, part])
+            if p == 0:
+                pieces = [pieces[i * 4 + zh * 2 + zl] for zh in range(2) for i in range(4) for zl in range(2)]
             tiles.append(jnp.concatenate(pieces, axis=0))
-        product = jnp.dot(
-            acts[:, pl.ds(pl.multiple_of(yy * 1280, 1280), 1280)],
-            jnp.concatenate(tiles, axis=1),
-            preferred_element_type=F32,
-        )
+        if p == 0:
+            left = acts[:, pl.ds(pl.multiple_of(at_outer * 1280, 1280), 1280)]
+        else:
+            left = acts_x[at_outer]
+        product = jnp.dot(left, jnp.concatenate(tiles, axis=1), preferred_element_type=F32)
         acc[p] = product if fresh else acc[p] + product
 
     def project_early(g):
-        add(g, 0, y, True)
+        for p in range(2):
+            add(g, p, outer[p], True)
 
         @pl.loop(0, 2)
         def _(k):
-            add(g, 0, lax.rem(y + 1 + 2 * k, 4))
+            for p in range(2):
+                add(g, p, lax.rem(outer[p] + 1 + 2 * k, 4))
 
     def project(g):
-        add(g, 0, turn(y, 2, 4))
-        add(g, 1, 0, True)
-
-        @pl.loop(1, 4)
-        def _(yy):
-            add(g, 1, yy)
-
-    def pack(g):
+        for p in range(2):
+            add(g, p, turn(outer[p], 2, 4))
+
+    def pack(to):
         peaks = []
         for head in range(4):
             p, lanes = head // 2, pl.ds(head % 2 * LANES, LANES)
@@ -372,25 +375,25 @@
             for page in range(4):
                 part = pl.ds(page * PAGE, PAGE)
                 k = head * 4 + page
-                stage[g, head, part] = (acc[p, part, lanes] * inverse[k : k + 1]).astype(BF16)
+                to[head, part] = (acc[p, part, lanes] * inverse[k : k + 1]).astype(BF16)
                 rows = jnp.where(row == page, scale[k : k + 1], rows)
-            stage[g, head, pl.ds(CHIP_TOKENS, 16)] = rows.astype(BF16)
+            to[head, pl.ds(CHIP_TOKENS, 16)] = rows.astype(BF16)
 
     def all_to_all(g):
         for d in range(3):
             send(
-                ("a2a", g, d), stage.at[g, far_chips[d]], pool_ref.at[z_lo], columns[d]
+                ("a2a", g, d), stage.at[far_chips[d]], pool_ref.at[z_lo], columns[d]
             )
-        send(("ahead", 1), stage.at[g, z_lo, UPPER], relay.at[0, UPPER], ahead)
-        send(("behind", 1), stage.at[g, z_lo, LOWER], relay.at[1, pl.ds(0, 256)], behind)
+        send(("ahead", 1), stage.at[z_lo, UPPER], relay.at[0, UPPER], ahead)
+        send(("behind", 1), stage.at[z_lo, LOWER], relay.at[1, pl.ds(0, 256)], behind)
         for d in (1, 2, 3):
             send(
                 ("across", d),
-                stage.at[g, jnp.bitwise_xor(z_lo, d)],
+                stage.at[jnp.bitwise_xor(z_lo, d)],
                 across_ref.at[z_lo],
                 opposite[d],
             )
-        own = pltpu.make_async_copy(stage.at[g, z_lo], pool_ref.at[z_lo], local_sem.at[4])
+        own = pltpu.make_async_copy(stage.at[z_lo], pool_ref.at[z_lo], local_sem.at[4])
         own.start()
         return own
 
@@ -439,7 +442,7 @@
             for head in range(4):
                 p, lanes = head // 2, pl.ds(head % 2 * LANES, LANES)
                 acc[p, part, lanes] = jnp.where(live(page), acc[p, part, lanes], 0.0)
-        pack(0)
+        pack(stage)
 
     def keys():
         project(1)
@@ -465,7 +468,7 @@
                 p, lanes = head // 2, pl.ds(head % 2 * LANES, LANES)
                 acc[p, part, lanes] = acc[p, part, lanes] * norm
         keep_fresh(0)
-        pack(1)
+        pack(stage_ref)
 
     V, K = 0, 1
     assemble(V)
@@ -501,6 +504,11 @@
     z_part(2, 3, V)
     outer_first(1, V)
     angles()
+    own_acts.wait()
+    for copy in own_decode:
+        copy.wait()
+    arrived("acts")
+    by_x(0)
     z_part(4, 0, V)
     z_part(3, 2, V)
     z_part(4, 0, K)
@@ -514,11 +522,14 @@
     z_part(2, 2, K)
     z_part(3, 1, K)
     outer_second(1, V)
+    by_x(1)
     z_part(4, 3, V)
+    by_x(2)
     z_part(2, 3, K)
     z_part(3, 2, K)
     z_part(4, 1, K)
     outer_second(2, V)
+    by_x(3)
     z_parts_done(V)
     outer_first(3, V)
     z_part(4, 2, K)
@@ -527,15 +538,12 @@
     outer_second(0, K)
     outer_second(3, V)
     outer_first(1, K)
-    own_acts.wait()
-    for copy in own_decode:
-        copy.wait()
-    arrived("acts")
+    by_x(4)
     project_early(V)
     outer_done(V)
     values()
+    own_values = all_to_all(V)
     outer_second(1, K)
-    own_values = all_to_all(V)
     outer_first(2, K)
     z_parts_done(K)
     outer_first(3, K)
@@ -544,10 +552,7 @@
     project_early(K)
     outer_done(K)
     keys()
-    stage_keys = pltpu.make_async_copy(stage.at[1], stage_ref, local_sem.at[6])
-    stage_keys.start()
     own_values.wait()
-    stage_keys.wait()
     for d in range(3):
         arrived(("a2a", V, d))
     for d in (1, 2, 3):
@@ -751,7 +756,7 @@
             jax.ShapeDtypeStruct((2, FRESH, LANES), BF16),
         ),
         in_specs=[pinned] * 8,
-        out_specs=(hbm, hbm, hbm, vmem),
+        out_specs=(hbm, hbm, vmem, vmem),
         scratch_shapes=[
             pltpu.VMEM((SHARD, 2 * HEADS * HEAD), BF16),
             pltpu.SMEM((16, 32), jnp.int32),
@@ -762,9 +767,10 @@
             pltpu.VMEM((2, 2, PADDED, 4 * LANES), BF16),
             pltpu.VMEM((2, 4, PADDED, 4 * LANES), BF16),
             pltpu.VMEM((ROWS, WIDTH), BF16),
+            pltpu.VMEM((4, ROWS, WIDTH // 4), BF16),
             pltpu.VMEM((2, 2, 4, 4, 4, BLOCK, LANES), BF16),
             pltpu.VMEM((2, ROWS, 2 * LANES), F32),
-            pltpu.VMEM((2, 4, SLAB, LANES), BF16),
+            pltpu.VMEM((4, SLAB, LANES), BF16),
             pltpu.VMEM((2, ROWS, LANES), F32),
             pltpu.VMEM((2, ROWS, LANES), F32),
             pltpu.VMEM((2, 272, LANES), BF16),
@@ -773,7 +779,7 @@
             pltpu.SemaphoreType.DMA((16,)),
         ],
         compiler_params=pltpu.CompilerParams(
-            collective_id=0, has_side_effects=True, vmem_limit_bytes=60 * 1024 * 1024
+            collective_id=0, has_side_effects=True, vmem_limit_bytes=57 * 1024 * 1024
         ),
     )(
         key_value_weight,

time: 111 us -> 112 us (level)
    pallas_call x1, Pallas kernels: 24.6 us -> 26.8 us  [on_device(): lax.switch(source_replica[0] - 1, [exchange_by(mask) for mask in range(1,...]
    pallas_call x1, Pallas kernels: 81.2 us -> 79.4 us  [on_device(): pl.pallas_call(gather_project, out_shape=(jax.ShapeDtypeStruct((4, SLAB,...]
where the time goes in v2:
time: 112 us
  Pallas kernels  110 us (98%)
  between operations  1.38 us (1%)
    pallas_call x1, Pallas kernels, on_device(): pl.pallas_call(gather_project, out_shape=(jax.ShapeDtypeStruct((4, SLAB,...  79.4 us
    pallas_call x1, Pallas kernels, on_device(): lax.switch(source_replica[0] - 1, [exchange_by(mask) for mask in range(1,...  26.8 us
    pallas_call x1, Pallas kernels, on_device(): pl.pallas_call(finish, out_shape=(jax.ShapeDtypeStruct((steps, paired, wi...  3.89 us

profile of v2, /device:TPU:6, one launch (start us, length us, event | category | flops | bytes accessed | tf_op | source)
XLA Modules:
  0.0 111.8 jit_solution(12887583660484356850)
XLA Ops:
  1.3 79.4 %shard_map.104 = (bf16[4,528,128]{2,1,0:T(8,128)(2,1)S(1)}, bf16[4,528,128]{2,1,0:T(8,128)(2,1)S(1)}, bf16[4,528,128]{2,1,0:T(8,128)(2,1)S(1)}, bf16[2,48,128]{2,1,0:T(8,128)(2,1)}) custom-call(bf16[20,2048]{1,0:T(8,128)(2,1)} %w_hbm.1, bf16[1,256,5120]{2,1,0:T(8,128)(2,1)} %prompt_ref.1, bf16[3,16,5120]{2,1,0:T(8,128)(2,1)} %decode_ref.1, ...), custom_call_target="tpu_custom_call" | custom-call | tf_op jit(solution)/shard_map/pallas_call | solution.py:750
  80.7 0.0 copy-start
  80.7 0.0 copy-start.1
  80.7 0.0 copy-start.2
  80.7 0.0 copy-start.3
  80.7 0.0 copy-start.4
  80.7 27.1 %conditional.1 = ((bf16[2,4,528,128]{3,2,1,0:T(8,128)(2,1)S(1)}, bf16[4,528,128]{2,1,0:T(8,128)(2,1)S(1)})) conditional(s32[]{:T(128)} %bitcast.1, (bf16[4,528,128]{2,1,0:T(8,128)(2,1)S(1)}, bf16[4,528,128]{2,1,0:T(8,128)(2,1)S(1)}, bf16[4,528,128]{2,1,0:T(8,128)(2,1)S(1)}) %tuple.100, ...), branch_computations={%region_0.0_spmd, %region_1.0_spmd, %region_2.0_spmd, %region_3.0_... | conditional | bytes 8 | solution.py:812
  81.0 26.8 %branch_27_fun.1 = (bf16[2,4,528,128]{3,2,1,0:T(8,128)(2,1)S(1)}, bf16[4,528,128]{2,1,0:T(8,128)(2,1)S(1)}) custom-call(bf16[4,528,128]{2,1,0:T(8,128)(2,1)S(1)} %get-tuple-element.267.pool_ref, bf16[4,528,128]{2,1,0:T(8,128)(2,1)S(1)} %get-tuple-element.268.across_ref, bf16[4,528,128]{2,1,0:T(8,128)(2,1)S(1)} %get-tuple-element.269.stage_ref), custom_call_target="tpu_custom_call" | custom-call | tf_op jit(solution)/shard_map/cond/branch_27_fun/pallas_call | solution.py:812
  107.8 0.0 copy-done
  107.8 0.0 copy-done.1
  107.9 0.0 copy-done.2
  107.9 0.0 copy-done.3
  107.9 0.0 copy-done.4
  107.9 3.9 %shard_map.105 = (bf16[3,16,640]{2,1,0:T(8,128)(2,1)}, f32[1,2,2048,128]{3,2,1,0:T(8,128)}) custom-call(bf16[3,16,640]{2,1,0:T(8,128)(2,1)S(1)} %copy-done, s32[16,32]{1,0:T(8,128)S(1)} %bitcast.5, s32[32]{0:T(128)S(1)} %copy-done.3, s32[32]{0:T(128)S(1)} %copy-done.4, bf16[4,528,128]{2,1,0:T(8,128)(2,1)S(1)} %get-tuple-element.290.keys_ref, ...), custom_call_target="tpu_custom_call" | custom-call | tf_op jit(solution)/shard_map/pallas_call | solution.py:820
Async XLA Ops:
  80.7 27.2 %copy-start = (bf16[3,16,640]{2,1,0:T(8,128)(2,1)S(1)}, bf16[3,16,640]{2,1,0:T(8,128)(2,1)}, u32[]{:S(2)}) copy-start(bf16[3,16,640]{2,1,0:T(8,128)(2,1)} %q_ref.1) | copy-start | bytes 184324
  80.7 27.2 %copy-start.1 = (s32[32,16]{0,1:T(8,128)S(1)}, s32[32,16]{0,1:T(8,128)}, u32[]{:S(2)}) copy-start(s32[32,16]{0,1:T(8,128)} %param.43) | copy-start | bytes 6148
  80.7 27.2 %copy-start.2 = (bf16[2,48,128]{2,1,0:T(8,128)(2,1)S(1)}, bf16[2,48,128]{2,1,0:T(8,128)(2,1)}, u32[]{:S(2)}) copy-start(bf16[2,48,128]{2,1,0:T(8,128)(2,1)} %get-tuple-element.292.fresh_ref) | copy-start | bytes 73732
  80.7 27.2 %copy-start.3 = (s32[32]{0:T(128)S(1)}, s32[32]{0:T(128)}, u32[]{:S(2)}) copy-start(s32[32]{0:T(128)} %length_ref.1) | copy-start | bytes 388
  80.7 27.2 %copy-start.4 = (s32[32]{0:T(128)S(1)}, s32[32]{0:T(128)}, u32[]{:S(2)}) copy-start(s32[32]{0:T(128)} %source_ref.1) | copy-start | bytes 388

commit v3 on v2

--- a/solution.py
+++ b/solution.py
@@ -38,7 +38,7 @@
 
 
 def gather_project(
-    w_hbm,
+    w_ref,
     prompt_ref,
     decode_ref,
     table_hbm,
@@ -50,7 +50,6 @@
     across_ref,
     stage_ref,
     fresh_ref,
-    w_ref,
     table_ref,
     length_ref,
     source_ref,
@@ -126,7 +125,6 @@
         pltpu.make_async_copy(src, dst, local_sem.at[8 + k])
         for k, (src, dst) in enumerate(
             [
-                (w_hbm, w_ref),
                 (table_hbm, table_ref),
                 (length_hbm, length_ref),
                 (source_hbm, source_ref),
@@ -152,21 +150,12 @@
     for copy in own_decode:
         copy.start()
 
-    small[0].wait()
-    keep = jnp.where(
-        lax.broadcasted_iota(jnp.int32, (PADDED, SHARD), 0)
-        == lax.broadcasted_iota(jnp.int32, (PADDED, SHARD), 1),
-        1.0,
-        0.0,
-    ).astype(BF16)
     for g in range(2):
         for c in range(2):
             tiles = [
                 w_ref[:, pl.ds((1 - g) * HEADS * HEAD + (2 * i + c) * HEAD, HEAD)] for i in range(4)
             ]
-            split[g, c] = jnp.dot(
-                keep, jnp.concatenate(tiles, axis=1), preferred_element_type=F32
-            ).astype(BF16)
+            split[g, c] = jnp.concatenate(tiles, axis=1)
         raw[g, odd * 2 + core] = split[g, core]
     pl.semaphore_wait(barrier, len(peers))
 
@@ -411,7 +400,7 @@
         return first(page) + line < length_ref[dp]
 
     def angles():
-        for copy in small[1:]:
+        for copy in small:
             copy.wait()
         for page in range(4):
             angle = (first(page) + line).astype(F32) * freq_ref[...]
@@ -755,10 +744,9 @@
             jax.ShapeDtypeStruct((4, SLAB, LANES), BF16),
             jax.ShapeDtypeStruct((2, FRESH, LANES), BF16),
         ),
-        in_specs=[pinned] * 8,
+        in_specs=[vmem] + [pinned] * 7,
         out_specs=(hbm, hbm, vmem, vmem),
         scratch_shapes=[
-            pltpu.VMEM((SHARD, 2 * HEADS * HEAD), BF16),
             pltpu.SMEM((16, 32), jnp.int32),
             pltpu.SMEM((32,), jnp.int32),
             pltpu.SMEM((32,), jnp.int32),
@@ -782,7 +770,7 @@
             collective_id=0, has_side_effects=True, vmem_limit_bytes=57 * 1024 * 1024
         ),
     )(
-        key_value_weight,
+        jnp.pad(key_value_weight, ((0, PADDED - SHARD), (0, 0))),
         prompt_hidden,
         decode_hidden,
         table,

time: 112 us -> 116 us (1.036)
  Pallas kernels: 110 us -> 113 us
  local copies, waits for them, and re-layouts: 0.03 us -> 1.59 us
    pallas_call x1, Pallas kernels: 26.8 us -> 29.4 us  [on_device(): lax.switch(source_replica[0] - 1, [exchange_by(mask) for mask in range(1,...]
    pad x0 -> x1, local copies, waits for them, and re-layouts: none -> 1.56 us  [on_device(): jnp.pad(key_value_weight, ((0, PADDED - SHARD), (0, 0)))]
where the time goes in v3:
time: 116 us; the launch traced here: 117 us
  Pallas kernels  113 us (97%)
  local copies, waits for them, and re-layouts  1.59 us (1%)
  between operations  1.38 us (1%)
    pallas_call x1, Pallas kernels, on_device(): pl.pallas_call(gather_project, out_shape=(jax.ShapeDtypeStruct((4, SLAB,...  80.2 us
    pallas_call x1, Pallas kernels, on_device(): lax.switch(source_replica[0] - 1, [exchange_by(mask) for mask in range(1,...  29.4 us
    pallas_call x1, Pallas kernels, on_device(): pl.pallas_call(finish, out_shape=(jax.ShapeDtypeStruct((steps, paired, wi...  3.89 us

profile of v3, /device:TPU:6, one launch (start us, length us, event | category | flops | bytes accessed | tf_op | source)
XLA Modules:
  0.0 116.7 jit_solution(10297927739231740830)
XLA Ops:
  1.3 1.6 %pad.4.w_ref = bf16[32,2048]{1,0:T(8,128)(2,1)} pad(bf16[20,2048]{1,0:T(8,128)(2,1)} %param.41, bf16[]{:T(256)} %constant.13.clone.1), padding=0_12x0_0 | pad | bytes 212994 | tf_op jit(solution)/shard_map/jit(_pad)/pad | solution.py:773
  2.8 80.2 %shard_map.104 = (bf16[4,528,128]{2,1,0:T(8,128)(2,1)S(1)}, bf16[4,528,128]{2,1,0:T(8,128)(2,1)S(1)}, bf16[4,528,128]{2,1,0:T(8,128)(2,1)S(1)}, bf16[2,48,128]{2,1,0:T(8,128)(2,1)}) custom-call(bf16[32,2048]{1,0:T(8,128)(2,1)} %pad.4.w_ref, bf16[1,256,5120]{2,1,0:T(8,128)(2,1)} %prompt_ref.1, bf16[3,16,5120]{2,1,0:T(8,128)(2,1)} %decode_ref.1, ...), custom_call_target="tpu_custom_call" | custom-call | tf_op jit(solution)/shard_map/pallas_call | solution.py:739
  83.0 0.0 copy-start
  83.0 0.0 copy-start.1
  83.1 0.0 copy-start.2
  83.1 0.0 copy-start.3
  83.1 0.0 copy-start.4
  83.1 29.7 %conditional.1 = ((bf16[2,4,528,128]{3,2,1,0:T(8,128)(2,1)S(1)}, bf16[4,528,128]{2,1,0:T(8,128)(2,1)S(1)})) conditional(s32[]{:T(128)} %bitcast.1, (bf16[4,528,128]{2,1,0:T(8,128)(2,1)S(1)}, bf16[4,528,128]{2,1,0:T(8,128)(2,1)S(1)}, bf16[4,528,128]{2,1,0:T(8,128)(2,1)S(1)}) %tuple.100, ...), branch_computations={%region_0.1_spmd, %region_1.2_spmd, %region_2.3_spmd, %region_3.4_... | conditional | bytes 8 | solution.py:800
  83.4 29.4 %branch_22_fun.1 = (bf16[2,4,528,128]{3,2,1,0:T(8,128)(2,1)S(1)}, bf16[4,528,128]{2,1,0:T(8,128)(2,1)S(1)}) custom-call(bf16[4,528,128]{2,1,0:T(8,128)(2,1)S(1)} %get-tuple-element.252.pool_ref, bf16[4,528,128]{2,1,0:T(8,128)(2,1)S(1)} %get-tuple-element.253.across_ref, bf16[4,528,128]{2,1,0:T(8,128)(2,1)S(1)} %get-tuple-element.254.stage_ref), custom_call_target="tpu_custom_call" | custom-call | tf_op jit(solution)/shard_map/cond/branch_22_fun/pallas_call | solution.py:800
  112.8 0.0 copy-done
  112.8 0.0 copy-done.1
  112.8 0.0 copy-done.2
  112.8 0.0 copy-done.3
  112.8 0.0 copy-done.4
  112.8 3.9 %shard_map.105 = (bf16[3,16,640]{2,1,0:T(8,128)(2,1)}, f32[1,2,2048,128]{3,2,1,0:T(8,128)}) custom-call(bf16[3,16,640]{2,1,0:T(8,128)(2,1)S(1)} %copy-done, s32[16,32]{1,0:T(8,128)S(1)} %bitcast.5, s32[32]{0:T(128)S(1)} %copy-done.3, s32[32]{0:T(128)S(1)} %copy-done.4, bf16[4,528,128]{2,1,0:T(8,128)(2,1)S(1)} %get-tuple-element.290.keys_ref, ...), custom_call_target="tpu_custom_call" | custom-call | tf_op jit(solution)/shard_map/pallas_call | solution.py:808
Async XLA Ops:
  83.0 29.7 %copy-start = (bf16[3,16,640]{2,1,0:T(8,128)(2,1)S(1)}, bf16[3,16,640]{2,1,0:T(8,128)(2,1)}, u32[]{:S(2)}) copy-start(bf16[3,16,640]{2,1,0:T(8,128)(2,1)} %q_ref.1) | copy-start | bytes 184324
  83.0 29.7 %copy-start.1 = (s32[32,16]{0,1:T(8,128)S(1)}, s32[32,16]{0,1:T(8,128)}, u32[]{:S(2)}) copy-start(s32[32,16]{0,1:T(8,128)} %param.43) | copy-start | bytes 6148
  83.1 29.7 %copy-start.2 = (bf16[2,48,128]{2,1,0:T(8,128)(2,1)S(1)}, bf16[2,48,128]{2,1,0:T(8,128)(2,1)}, u32[]{:S(2)}) copy-start(bf16[2,48,128]{2,1,0:T(8,128)(2,1)} %get-tuple-element.292.fresh_ref) | copy-start | bytes 73732
  83.1 29.7 %copy-start.3 = (s32[32]{0:T(128)S(1)}, s32[32]{0:T(128)}, u32[]{:S(2)}) copy-start(s32[32]{0:T(128)} %length_ref.1) | copy-start | bytes 388
  83.1 29.7 %copy-start.4 = (s32[32]{0:T(128)S(1)}, s32[32]{0:T(128)}, u32[]{:S(2)}) copy-start(s32[32]{0:T(128)} %source_ref.1) | copy-start | bytes 388
